TPU v7x, 128 devices: a whole 4x4x4 slice. The times are simulated.
128 devices in a mesh: frame: 8 (over x, core), cell: 16 (over y, z).
Axes of the slice: x: 4, y: 4, z: 4, core: 2. Of those that a mesh axis runs over, the one named last changes fastest.
Arguments:
- front: float32 [8, 4096, 4096], P('frame', 'cell')
- parent_of: int32 [8], replicated, may hold values from 0 to 7
- block_map: int32 [8, 13], replicated, may hold values from 3 to 31, as said below
- parent_in: bfloat16 [8, 2, 4096, 8192], P('frame', None, 'cell'), may hold values from -0.3125 to 0.3125
Outputs:
- lower_panel: float32 [8, 4096, 768], P('frame', 'cell')
- parent_out: bfloat16 [8, 2, 4096, 8192], P('frame', None, 'cell')
Inputs may be any that keep to these rules, and one draw needn't show every extreme that they name: block_map[c, k] is 3 + k or 3 + k + 16.
All inputs are finite; a program needn't handle non-finite values.
Results may differ from a plain program's by a relative error of at most 0.004.
Values may be sent and summed in bfloat16 or wider, within the bound.
A program may use at most 192 MiB of HBM per device.

v0:
```python
import jax
import jax.numpy as jnp
from jax import lax
from jax.sharding import PartitionSpec as P

PB = 3


def per_device(front, parent_of, block_map, parent_in):
    block_row = front[0]
    rows_here = block_row.shape[0]
    order = block_row.shape[1]
    blocks = order // rows_here
    width = PB * rows_here
    cell_index = lax.axis_index("cell")
    frame_index = lax.axis_index("frame")
    highest = lax.Precision.HIGHEST
    panel = lax.all_gather(block_row[:, :width], "cell", axis=0, tiled=True)
    l11 = jnp.linalg.cholesky(panel[:width])
    l21 = lax.linalg.triangular_solve(
        l11, panel[width:], left_side=False, lower=True, transpose_a=True
    )
    lower_all = jnp.concatenate([l11, l21], 0)
    my_lower = lax.dynamic_slice_in_dim(lower_all, cell_index * rows_here, rows_here, 0)
    product = jnp.dot(my_lower, l21.T, precision=highest)
    update = (block_row[:, width:] - product).astype(jnp.bfloat16)
    update_blocks = update.shape[1] // rows_here
    which_k = jnp.maximum(cell_index - PB, 0)
    whole_parent = parent_in[0].reshape(2, rows_here, 2, blocks, rows_here)
    region_start = whole_parent[:, :, :, PB:, :].astype(jnp.float32)
    pieces = lax.all_gather(update[None], "frame", axis=0, tiled=True)

    def one_child(step, acc):
        parent = lax.dynamic_index_in_dim(parent_of, step, 0, keepdims=False)
        positions = lax.dynamic_index_in_dim(block_map, step, 0, keepdims=False)
        target = lax.dynamic_index_in_dim(positions, which_k, 0, keepdims=False)
        live = (parent == frame_index) & (cell_index >= PB)
        half = target // blocks

        def add_piece(inner):
            piece = lax.dynamic_index_in_dim(pieces, step, 0, keepdims=False)
            piece = piece.reshape(rows_here, update_blocks, rows_here).astype(jnp.float32)
            upper = (positions >= blocks)[None, :, None]
            zeros = jnp.zeros_like(piece)
            delta = jnp.stack([jnp.where(upper, zeros, piece), jnp.where(upper, piece, zeros)], 1)
            current = lax.dynamic_index_in_dim(inner, half, 0, keepdims=False)
            return lax.dynamic_update_index_in_dim(inner, current + delta, half, 0)

        def keep_same(inner):
            return inner

        return lax.cond(live, add_piece, keep_same, acc)

    total = lax.fori_loop(0, pieces.shape[0], one_child, region_start)
    merged = jnp.concatenate([whole_parent[:, :, :, :PB, :], total.astype(jnp.bfloat16)], 3)
    merged = merged.reshape(2, rows_here, 2 * blocks * rows_here)
    return (my_lower[None], merged[None])


def solution(mesh):
    placed = (P("frame", "cell", None), P(), P(), P("frame", None, "cell", None))
    return jax.shard_map(
        per_device,
        mesh=mesh,
        in_specs=placed,
        out_specs=(P("frame", "cell", None), P("frame", None, "cell", None)),
        check_vma=False,
    )
```

profile of v0, /device:TPU:15, one launch (start us, length us, event | category | flops | bytes accessed | tf_op | source)
XLA Modules:
  0.0 594.5 jit_solution(12432647070224209038)
XLA Ops:
  15.0 101.0 %all-gather.4.cloned.1.call-done = f32[4096,768]{0,1:T(8,128)} async-done(((f32[256,768]{0,1:T(8,128)}), f32[4096,768]{0,1:T(8,128)}) %all-gather.4.cloned.1.call-update) | async-done | bytes 12582928 | tf_op jit(solution)/shard_map/all_gather | solution.py:18
  123.7 11.7 %cholesky.165 = f32[128,128]{1,0:T(8,128)S(1)} custom-call(f32[128,128]{1,0:T(8,128)S(1)} %cholesky.424), custom_call_target="Cholesky" | custom-call | tf_op jit(solution)/shard_map/jit(cholesky)/cholesky | solution.py:19
  135.4 9.8 %custom-call.46 = f32[1,128,128]{1,2,0:T(8,128)S(1)} custom-call(f32[1,128,128]{2,1,0:T(8,128)S(1)} %get-tuple-element.497), custom_call_target="InvertDiagBlocksLowerTriangular" | custom-call | tf_op jit(solution)/shard_map/jit(cholesky)/cholesky | solution.py:19
  148.2 11.7 %cholesky.188 = f32[128,128]{1,0:T(8,128)S(1)} custom-call(f32[128,128]{1,0:T(8,128)S(1)} %cholesky.428), custom_call_target="Cholesky" | custom-call | tf_op jit(solution)/shard_map/jit(cholesky)/cholesky | solution.py:19
  160.0 10.1 %custom-call.47 = f32[1,128,128]{1,2,0:T(8,128)S(1)} custom-call(f32[1,128,128]{2,1,0:T(8,128)S(1)} %get-tuple-element.494), custom_call_target="InvertDiagBlocksLowerTriangular" | custom-call | tf_op jit(solution)/shard_map/jit(cholesky)/cholesky | solution.py:19
  172.0 11.7 %cholesky.354 = f32[128,128]{1,0:T(8,128)S(1)} custom-call(f32[128,128]{1,0:T(8,128)S(1)} %cholesky.433), custom_call_target="Cholesky" | custom-call | tf_op jit(solution)/shard_map/jit(cholesky)/cholesky | solution.py:19
  184.4 9.8 %custom-call.48 = f32[1,128,128]{1,2,0:T(8,128)S(1)} custom-call(f32[1,128,128]{2,1,0:T(8,128)S(1)} %get-tuple-element.491), custom_call_target="InvertDiagBlocksLowerTriangular" | custom-call | tf_op jit(solution)/shard_map/jit(cholesky)/cholesky | solution.py:19
  196.1 11.9 %cholesky.373 = f32[128,128]{1,0:T(8,128)S(1)} custom-call(f32[128,128]{1,0:T(8,128)S(1)} %cholesky.438), custom_call_target="Cholesky" | custom-call | tf_op jit(solution)/shard_map/jit(cholesky)/cholesky | solution.py:19
  208.7 9.8 %custom-call.49 = f32[1,128,128]{1,2,0:T(8,128)S(1)} custom-call(f32[1,128,128]{2,1,0:T(8,128)S(1)} %get-tuple-element.488), custom_call_target="InvertDiagBlocksLowerTriangular" | custom-call | tf_op jit(solution)/shard_map/jit(cholesky)/cholesky | solution.py:19
  220.3 11.7 %cholesky.392 = f32[128,128]{1,0:T(8,128)S(1)} custom-call(f32[128,128]{1,0:T(8,128)S(1)} %cholesky.443), custom_call_target="Cholesky" | custom-call | tf_op jit(solution)/shard_map/jit(cholesky)/cholesky | solution.py:19
  232.7 9.8 %custom-call.50 = f32[1,128,128]{1,2,0:T(8,128)S(1)} custom-call(f32[1,128,128]{2,1,0:T(8,128)S(1)} %get-tuple-element.485), custom_call_target="InvertDiagBlocksLowerTriangular" | custom-call | tf_op jit(solution)/shard_map/jit(cholesky)/cholesky | solution.py:19
  244.0 12.1 %cholesky.410 = f32[128,128]{1,0:T(8,128)S(1)} custom-call(f32[128,128]{1,0:T(8,128)S(1)} %convolution_subtract_fusion.8), custom_call_target="Cholesky" | custom-call | tf_op jit(solution)/shard_map/jit(cholesky)/cholesky | solution.py:19
  263.5 17.4 %while.21 = (s32[]{:T(128)}, f32[768,768]{1,0:T(8,128)}, s32[6,2]{0,1:T(2,128)S(1)}, f32[6,128,128]{2,1,0:T(8,128)S(1)}, s32[]{:T(128)}) while((s32[]{:T(128)}, f32[768,768]{1,0:T(8,128)}, s32[6,2]{0,1:T(2,128)S(1)}, f32[6,128,128]{2,1,0:T(8,128)S(1)}, s32[]{:T(128)}) %tuple.115), condition=%wide.while_cond, body=%wide.while_body.sunk | while | flops 2 | bytes 131181 | solution.py:20
  281.0 59.0 %custom-call.51 = f32[6,128,128]{1,2,0:T(8,128)S(1)} custom-call(f32[6,128,128]{2,1,0:T(8,128)S(1)} %get-tuple-element.425), custom_call_target="InvertDiagBlocksLowerTriangular" | custom-call | tf_op jit(solution)/shard_map/triangular_solve | solution.py:20
  393.8 18.2 %fusion.9 = bf16[256,3328]{0,1:T(8,128)(2,1)} fusion(f32[256,768]{0,1:T(8,128)S(1)} %fusion.29, f32[3328,768]{0,1:T(8,128)S(1)} %convolution_dynamic-update-slice_fusion, f32[256,4096]{0,1:T(8,128)S(1)} %bitcast.109), kind=kOutput, calls=%fused_computation.24 | convolution fusion | flops 7853441024 | bytes 16121856 | tf_op jit(solution)/shard_map/dot_general | solution.py:25
  412.0 12.0 %copy.15 = bf16[1,2,256,8192]{2,3,1,0:T(8,128)(2,1)} copy(bf16[1,2,256,8192]{3,2,1,0:T(8,128)(2,1)} %param.11) | data formatting | bytes 16777216 | tf_op args[3]
  425.7 9.8 %slice_convert_fusion = f32[2,256,2,13,256]{1,4,3,2,0:T(8,128)} fusion(bf16[2,256,2,16,256]{1,4,3,2,0:T(8,128)(2,1)} %bitcast.103), kind=kLoop, calls=%fused_computation.13 | loop fusion | flops 3407872 | bytes 20447232 | tf_op jit(solution)/shard_map/convert_element_type | solution.py:30
  436.7 52.1 %all-gather.6.cloned.1.call-done = bf16[2048,3328]{0,1:T(8,128)(2,1)} async-done(((bf16[256,3328]{0,1:T(8,128)(2,1)}), bf16[2048,3328]{0,1:T(8,128)(2,1)}) %all-gather.6.cloned.1.call-update) | async-done | bytes 13631504 | tf_op jit(solution)/shard_map/all_gather | solution.py:31
  488.8 12.5 %copy.23 = bf16[416,8,8,256]{3,2,0,1:T(8,128)(2,1)} copy(bf16[416,8,8,256]{3,2,1,0:T(8,128)(2,1)} %bitcast.112) | data formatting | bytes 27262976 | tf_op jit(solution)/shard_map/all_gather | solution.py:31
  501.3 58.4 %while.20 = (s32[]{:T(128)}, f32[2,256,2,13,256]{1,4,3,2,0:T(8,128)}, s32[8]{0:T(128)S(1)}, s32[]{:T(128)}, pred[]{:T(512)}, /*index=5*/s32[8,13]{1,0:T(8,128)},...) while((s32[]{:T(128)}, f32[2,256,2,13,256]{1,4,3,2,0:T(8,128)}, ...), condition=%wide.region_15.16_spmd, body=%wide.region_12.15_spmd.sunk | while | flops 5963816 | bytes 32375320 | solution.py:54
  506.7 12.5 %conditional.2 = (f32[2,256,2,13,256]{1,4,3,2,0:T(8,128)}) conditional(s32[]{:T(128)} %convert_element_type.50, f32[2,256,2,13,256]{1,4,3,2,0:T(8,128)} %get-tuple-element.611, (s32[]{:T(128)}, s32[]{:T(128)}, f32[2,256,2,13,256]{1,4,3,2,0:T(8,128)}, s32[8,13]{1,0:T(8,128)}, s32[]{:T(128)}, /*index=5*/bf16[8,256,3328]{1,2,0:T(8,128)(2,1)}, ...), branch_computations={%region_13.13_spmd, %region_14.14_spmd} | conditional | flops 5963810 | bytes 32375100 | solution.py:52
  521.7 12.5 %conditional.2 = (f32[2,256,2,13,256]{1,4,3,2,0:T(8,128)}) conditional(s32[]{:T(128)} %convert_element_type.50, f32[2,256,2,13,256]{1,4,3,2,0:T(8,128)} %get-tuple-element.611, (s32[]{:T(128)}, s32[]{:T(128)}, f32[2,256,2,13,256]{1,4,3,2,0:T(8,128)}, s32[8,13]{1,0:T(8,128)}, s32[]{:T(128)}, /*index=5*/bf16[8,256,3328]{1,2,0:T(8,128)(2,1)}, ...), branch_computations={%region_13.13_spmd, %region_14.14_spmd} | conditional | flops 5963810 | bytes 32375100 | solution.py:52
  547.2 12.5 %conditional.2 = (f32[2,256,2,13,256]{1,4,3,2,0:T(8,128)}) conditional(s32[]{:T(128)} %convert_element_type.50, f32[2,256,2,13,256]{1,4,3,2,0:T(8,128)} %get-tuple-element.611, (s32[]{:T(128)}, s32[]{:T(128)}, f32[2,256,2,13,256]{1,4,3,2,0:T(8,128)}, s32[8,13]{1,0:T(8,128)}, s32[]{:T(128)}, /*index=5*/bf16[8,256,3328]{1,2,0:T(8,128)(2,1)}, ...), branch_computations={%region_13.13_spmd, %region_14.14_spmd} | conditional | flops 5963810 | bytes 32375100 | solution.py:52
  575.3 12.0 %copy.20 = bf16[1,2,256,8192]{3,2,1,0:T(8,128)(2,1)} copy(bf16[1,2,256,8192]{2,3,1,0:T(8,128)(2,1)} %bitcast.104) | data formatting | bytes 16777216 | tf_op jit(solution)/shard_map/broadcast_in_dim;reshape | solution.py:57
  (128 shorter events, 165.5 us)
Async XLA Ops:
  7.2 108.8 %all-gather.4.cloned.1.call-start = ((), (), s32[]{:S(2)}) async-start(), calls=%async_computation | async-start | bytes 13369344 | tf_op jit(solution)/shard_map/all_gather | solution.py:18
  14.9 473.9 %all-gather.6.cloned.1.call-start = ((), (), s32[]{:S(2)}) async-start(), calls=%async_computation.1 | async-start | bytes 15335424 | tf_op jit(solution)/shard_map/all_gather | solution.py:31
  115.9 1.7 slice-start.3
  122.3 1.4 copy-start.3
  339.9 8.6 %copy-start.4 = (f32[6,128,128]{1,2,0:T(8,128)}, f32[6,128,128]{1,2,0:T(8,128)S(1)}, u32[]{:S(2)}) copy-start(f32[6,128,128]{1,2,0:T(8,128)S(1)} %custom-call.51) | copy-start | bytes 1179652
  345.2 14.6 %slice-start = ((s8[12582912]{0:T(1024)(128)(4,1)}), s8[4194304]{0:T(1024)(128)(4,1)S(1)}, s32[]{:S(2)}) async-start(s8[12582912]{0:T(1024)(128)(4,1)} %bitcast.110), calls=%async_computation.2 | async-start | bytes 8388608
  348.5 11.3 %slice-start.1 = ((s8[12582912]{0:T(1024)(128)(4,1)}), s8[4194304]{0:T(1024)(128)(4,1)S(1)}, s32[]{:S(2)}) async-start(s8[12582912]{0:T(1024)(128)(4,1)} %bitcast.110), calls=%async_computation.3 | async-start | bytes 8388608
  350.3 9.6 %slice-start.2 = ((s8[12582912]{0:T(1024)(128)(4,1)}), s8[4194304]{0:T(1024)(128)(4,1)S(1)}, s32[]{:S(2)}) async-start(s8[12582912]{0:T(1024)(128)(4,1)} %bitcast.110), calls=%async_computation.4 | async-start | bytes 8388608
  356.6 3.2 copy-start.1
  359.9 5.0 copy-start.2
  391.6 2.2 copy-start
  488.8 12.5 %copy-start.5 = (s32[8]{0:T(128)S(1)}, s32[8]{0:T(128)}, u32[]{:S(2)}) copy-start(s32[8]{0:T(128)} %param.9) | copy-start | bytes 100
Sparse Core Ops, SparseCore 0:
  15.0 100.8 all-gather.3
  412.1 76.6 all-gather.5
where the time goes:
time: 606 us; the launch traced here: 594 us
  other arithmetic  238 us (39%)
  waiting for transfers between devices  153 us (25%)
  local copies, waits for them, and re-layouts  97.1 us (16%)
  matrix products  74 us (12%)
  between operations  18.5 us (3%)
  loops' own time  14 us (2%)
    another operation x22, other arithmetic, per_device(): l11 = jnp.linalg.cholesky(panel[:width])  124 us
    all_gather x1, waiting for transfers between devices, per_device(): panel = lax.all_gather(block_row[:, :width], 'cell', axis=0, tiled=True)  101 us
    another operation x3, other arithmetic, per_device(): lax.linalg.triangular_solve(l11, panel[width:], left_side=False, lower=Tr...  61.4 us
    all_gather x1, waiting for transfers between devices, per_device(): pieces = lax.all_gather(update[None], 'frame', axis=0, tiled=True)  52.1 us
    another operation x11, matrix products, per_device(): lax.linalg.triangular_solve(l11, panel[width:], left_side=False, lower=Tr...  46.1 us
    unnamed x20, local copies, waits for them, and re-layouts  24.3 us
    dynamic_update_slice x3, other arithmetic, add_piece(): return lax.dynamic_update_index_in_dim(inner, current + delta, half, 0)  19.8 us
    dot_general x1, matrix products, per_device(): product = jnp.dot(my_lower, l21.T, precision=highest)  18.2 us
  transfers between devices with their start and end apart: 2, of which 2 were waited for; matrix products, arithmetic and copies ran while one was open for 4% of the time, Pallas kernels for 0%

commit v1 on v0

v1 whole, which is shorter than its diff:
```python
import functools

import jax
import jax.numpy as jnp
from jax import lax
from jax.experimental import pallas as pl
from jax.experimental.pallas import tpu as pltpu
from jax.sharding import PartitionSpec as P

PB = 3
BLK = 256
F32, BF16 = jnp.float32, jnp.bfloat16
NT = (((1,), (1,)), ((), ()))
TN = (((0,), (0,)), ((), ()))
STRIP = 16
SIDE = 4
CELLS = SIDE * SIDE
FRAMES = 2 * SIDE
WIDTH = PB * BLK
OFFSET = (0, BLK, 3 * BLK)
PACKED = 6 * BLK
PART = BLK // CELLS
VMEM = pltpu.VMEM
DMA = pltpu.SemaphoreType.DMA
MESH = pl.DeviceIdType.MESH


def remote(src, dst, send, recv, frame, cell):
    return pltpu.make_async_remote_copy(
        src_ref=src, dst_ref=dst, send_sem=send, recv_sem=recv,
        device_id=(frame, cell), device_id_type=MESH,
    )


def greet(devices):
    barrier = pltpu.get_barrier_semaphore()
    for frame, cell in devices:
        pl.semaphore_signal(barrier, inc=1, device_id=(frame, cell), device_id_type=MESH)
    pl.semaphore_wait(barrier, len(devices))


def pivot_kernel(front, packed, part, send1, recv1, local1, send2, recv2, local2):
    frame, cell = lax.axis_index("frame"), lax.axis_index("cell")
    greet([(frame, lax.rem(cell + i, CELLS)) for i in range(1, CELLS)])

    def scatter(r, d):
        wide = BLK * (r + 1)
        src = front.at[pl.ds(pl.multiple_of(d * PART, PART), PART), pl.ds(0, wide)]
        return src, part.at[:, pl.ds(OFFSET[r], wide)]

    for r in range(PB):
        @pl.when(cell == r)
        def _(r=r):
            for i in range(1, CELLS):
                d = lax.rem(r + i, CELLS)
                src, dst = scatter(r, d)
                remote(src, dst, send1.at[i], recv1.at[r], frame, d).start()
            src, dst = scatter(r, r)
            own = pltpu.make_async_copy(src, dst, local1)
            own.start()
            own.wait()

    for r in range(PB):
        @pl.when(cell != r)
        def _(r=r):
            src, dst = scatter(r, cell)
            remote(src, dst, send1.at[0], recv1.at[r], frame, r).wait_recv()

    keep = pltpu.make_async_copy(part, packed.at[cell], local2)
    keep.start()
    for i in range(1, CELLS):
        d = lax.rem(cell + i, CELLS)
        remote(part, packed.at[cell], send2.at[i], recv2.at[cell], frame, d).start()
    for i in range(1, CELLS):
        d = lax.rem(cell + i, CELLS)
        remote(part, packed.at[d], send2.at[i], recv2.at[d], frame, d).wait()
    keep.wait()
    for r in range(PB):
        @pl.when(cell == r)
        def _(r=r):
            for i in range(1, CELLS):
                d = lax.rem(r + i, CELLS)
                src, dst = scatter(r, d)
                remote(src, dst, send1.at[i], recv1.at[r], frame, d).wait_send()


def gather_pivot(front):
    return pl.pallas_call(
        pivot_kernel,
        out_shape=jax.ShapeDtypeStruct((CELLS, PART, PACKED), F32),
        in_specs=[pl.BlockSpec(memory_space=pl.ANY)],
        out_specs=pl.BlockSpec(memory_space=pl.ANY),
        scratch_shapes=[
            VMEM((PART, PACKED), F32),
            DMA((CELLS,)), DMA((PB,)), DMA, DMA((CELLS,)), DMA((CELLS,)), DMA,
        ],
        compiler_params=pltpu.CompilerParams(collective_id=1, has_side_effects=True),
        name="gather_pivot",
    )(front)


def split(x):
    hi = x.astype(BF16)
    return hi, (x - hi.astype(F32)).astype(BF16)


def dot3(a, b, dims):
    def one(u, v):
        return lax.dot_general(u, v, dims, preferred_element_type=F32)

    return one(a[0], b[0]) + one(a[0], b[1]) + one(a[1], b[0])


def strip_step(s, work, done):
    first = pl.multiple_of(s * STRIP, STRIP)
    rows = work[pl.ds(first, STRIP), :]
    left, right = rows[:, :128], rows[:, 128:]
    turned = pltpu.roll(left, lax.rem(128 - first, 128), 1)
    cols = [jnp.broadcast_to(turned[:, b:b + 1], (STRIP, 128)) for b in range(STRIP)]
    row_no = lax.broadcasted_iota(jnp.int32, (STRIP, 128), 0)
    lane = lax.broadcasted_iota(jnp.int32, (STRIP, 128), 1)
    scale = jnp.zeros((STRIP, 128), F32)
    for a in range(STRIP):
        below = jnp.where(row_no > a, cols[a], 0.0)
        root = jnp.broadcast_to(lax.rsqrt(cols[a][a:a + 1, :]), (STRIP, 128))
        over = root * root
        scale = jnp.where(row_no == a, root, scale)
        if a < STRIP - 1:
            for b in range(a + 1, STRIP):
                cols[b] = cols[b] - (below * cols[b][a:a + 1, :]) * over
            ratio = below * over
            left = left - ratio * left[a:a + 1, :]
            right = right - ratio * right[a:a + 1, :]
    upper = jnp.where(lane >= row_no + first, left * scale, 0.0)
    inverse = right * scale
    done[pl.ds(first, STRIP), :128] = upper
    done[pl.ds(first, STRIP), 128:] = inverse
    u1, u2 = split(upper)
    v1, v2 = split(inverse)
    one, two = jnp.concatenate([u1, v1], 1), jnp.concatenate([u2, v2], 1)
    work[...] -= lax.dot_general(
        jnp.concatenate([u1, u1, u2], 0), jnp.concatenate([one, two, one], 0), TN,
        preferred_element_type=F32,
    )


def factor_kernel(where_ref, packed, own, lower, panel, a, work, done):
    for r in range(PB):
        a[BLK * r:BLK * (r + 1), :BLK * (r + 1)] = packed[:, OFFSET[r]:OFFSET[r] + BLK * (r + 1)]
    a[WIDTH:] = own[...]
    blocks = WIDTH // 128
    eye = (
        lax.broadcasted_iota(jnp.int32, (128, 128), 0)
        == lax.broadcasted_iota(jnp.int32, (128, 128), 1)
    ).astype(F32)
    for j in range(blocks):
        lo, hi = 128 * j, 128 * (j + 1)
        work[:, :128] = a[lo:hi, lo:hi]
        work[:, 128:] = eye

        def step(s, carry):
            strip_step(s, work, done)
            return carry

        lax.fori_loop(0, 128 // STRIP, step, 0)
        inverse = split(done[:, 128:])
        a[lo:hi, lo:hi] = done[:, :128].T
        below = dot3(split(a[hi:, lo:hi]), inverse, NT)
        a[hi:, lo:hi] = below
        p1, p2 = split(below)
        for k in range(j + 1, blocks):
            o = 128 * (k - j - 1)
            a[128 * k:, 128 * k:128 * (k + 1)] -= dot3(
                (p1[o:], p2[o:]), (p1[o:o + 128], p2[o:o + 128]), NT
            )
    start = pl.multiple_of(where_ref[0], BLK)
    mine = a[pl.ds(start, BLK), :]
    row_no = lax.broadcasted_iota(jnp.int32, (BLK, WIDTH), 0) + start
    col_no = lax.broadcasted_iota(jnp.int32, (BLK, WIDTH), 1)
    lower[...] = jnp.where(row_no >= col_no, mine, 0.0)
    panel[...] = a[WIDTH:].astype(BF16)


def factor(where, packed, own):
    spec = pl.BlockSpec(memory_space=VMEM)
    return pl.pallas_call(
        factor_kernel,
        out_shape=(
            jax.ShapeDtypeStruct((BLK, WIDTH), F32),
            jax.ShapeDtypeStruct((BLK, WIDTH), BF16),
        ),
        in_specs=[pl.BlockSpec(memory_space=pltpu.SMEM), spec, spec],
        out_specs=(spec, spec),
        scratch_shapes=[
            VMEM((WIDTH + BLK, WIDTH), F32), VMEM((128, 256), F32), VMEM((128, 256), F32),
        ],
        compiler_params=pltpu.CompilerParams(vmem_limit_bytes=40 << 20),
        name="factor",
    )(where, packed, own)


LAG, LAG2, STEPS = 2, 4, CELLS


def update_kernel(
    panel, front, pieces, held, rest, chunk, rest_sem,
    dsend, drecv, asend, arecv, bsend, brecv, xsend, xrecv, keep_sem,
):
    frame, cell = lax.axis_index("frame"), lax.axis_index("cell")
    x, core = frame // 2, lax.rem(frame, 2)
    y, z = cell // SIDE, lax.rem(cell, SIDE)
    right = lax.rem(x + 1, SIDE) * 2 + core
    left = lax.rem(x + SIDE - 1, SIDE) * 2 + core
    across = lax.rem(x + 2, SIDE) * 2 + core
    sibling = x * 2 + 1 - core
    has_rows = cell >= PB
    load = pltpu.make_async_copy(front.at[:, pl.ds(WIDTH, CELLS * BLK - WIDTH)], rest, rest_sem)

    @pl.when(has_rows)
    def _():
        load.start()

    held[cell] = panel[...]

    def row_peer(i):
        return y * SIDE + lax.rem(z + i, SIDE)

    def col_peer(i):
        return lax.rem(y + i, SIDE) * SIDE + z

    greet(
        [(frame, row_peer(i)) for i in range(1, SIDE)]
        + [(frame, col_peer(i)) for i in range(1, SIDE)]
        + [(left, cell), (right, cell), (sibling, cell)]
    )

    def direct(slot, src, to):
        return remote(held.at[src], held.at[src], dsend.at[slot], drecv.at[src], frame, to)

    def half_a(slot, src, to):
        part = held.at[src, pl.ds(0, 128)]
        return remote(part, part, asend.at[slot], arecv.at[src], frame, to)

    def half_b(slot, src, to):
        part = held.at[src, pl.ds(128, 128)]
        return remote(part, part, bsend.at[slot], brecv.at[src], frame, to)

    @pl.when(has_rows)
    def _():
        for i in (1, 3, 2):
            direct(i - 1, cell, row_peer(i)).start()
            direct(i + 2, cell, col_peer(i)).start()

    def order(t):
        i, by_row = 1 + (t - 1) // 2, lax.rem(t - 1, 2) == 0
        u = t - 7
        dy = jnp.where(t == 0, 0, jnp.where(t < 7, jnp.where(by_row, 0, i), 1 + u // 3))
        dz = jnp.where(t == 0, 0, jnp.where(t < 7, jnp.where(by_row, i, 0), 1 + lax.rem(u, 3)))
        return lax.rem(y + dy, SIDE) * SIDE + lax.rem(z + dz, SIDE)

    def x_copy(kind, c):
        whole = pl.ds(0, BLK)
        source, rows, to = [
            (frame, whole, right), (frame, whole, left), (frame, whole, sibling),
            (left, pl.ds(0, 128), right), (left, whole, sibling),
            (right, pl.ds(128, 128), left), (right, whole, sibling),
            (across, whole, sibling),
        ][kind]
        dst = pieces.at[source, c, rows]
        src = chunk.at[c, rows] if kind < 3 else dst
        return remote(src, dst, xsend.at[kind, c], xrecv.at[kind, c], to, cell)

    def keep(c):
        return pltpu.make_async_copy(chunk.at[c], pieces.at[frame, c], keep_sem.at[c])

    def step(t, carry):
        c = order(t)

        @pl.when((t < STEPS) & (c >= PB))
        def _():
            by_row = lax.rem(t - 1, 2) == 0

            @pl.when((t >= 1) & (t < 7))
            def _():
                direct(0, c, cell).wait_recv()

                @pl.when(by_row)
                def _():
                    for i in (1, 3, 2):
                        @pl.when(col_peer(i) >= PB)
                        def _(i=i):
                            half_a((t - 1) // 2 * 3 + i - 1, c, col_peer(i)).start()

                @pl.when(jnp.logical_not(by_row))
                def _():
                    for i in (1, 3, 2):
                        @pl.when(row_peer(i) >= PB)
                        def _(i=i):
                            half_b((t - 1) // 2 * 3 + i - 1, c, row_peer(i)).start()

            @pl.when(has_rows)
            def _():
                @pl.when(t == 0)
                def _():
                    load.wait()

                @pl.when(t >= 7)
                def _():
                    half_a(0, c, cell).wait_recv()
                    half_b(0, c, cell).wait_recv()

                product = lax.dot_general(panel[...], held[c], NT, preferred_element_type=F32)
                base = rest[:, pl.ds(pl.multiple_of((c - PB) * BLK, BLK), BLK)]
                chunk[c] = (base - product).astype(BF16)
                keep(c).start()
                for kind in range(3):
                    x_copy(kind, c).start()

        back = order(t - LAG)

        @pl.when((t >= LAG) & (t < STEPS + LAG) & has_rows & (back >= PB))
        def _():
            recv(0, left, pl.ds(0, BLK), back)
            x_copy(3, back).start()
            x_copy(4, back).start()
            recv(1, right, pl.ds(0, BLK), back)
            x_copy(5, back).start()
            x_copy(6, back).start()

        far = order(t - LAG2)

        @pl.when((t >= LAG2) & has_rows & (far >= PB))
        def _():
            recv(3, across, pl.ds(0, 128), far)
            recv(5, across, pl.ds(128, 128), far)
            x_copy(7, far).start()

        return carry

    def recv(kind, source, rows, c):
        dst = pieces.at[source, c, rows]
        remote(dst, dst, xsend.at[kind, c], xrecv.at[kind, c], sibling, cell).wait_recv()

    lax.fori_loop(0, STEPS + LAG2, step, 0)

    def finish(t, carry):
        @pl.when(has_rows & (t >= PB))
        def _():
            whole = pl.ds(0, BLK)
            recv(2, sibling, whole, t)
            other = 1 - 2 * core
            recv(4, left + other, whole, t)
            recv(6, right + other, whole, t)
            recv(7, across + other, whole, t)
            keep(t).wait()
            for kind in range(8):
                x_copy(kind, t).wait_send()

        return carry

    lax.fori_loop(0, CELLS, finish, 0)

    @pl.when(has_rows)
    def _():
        for i in range(1, SIDE):
            direct(i - 1, cell, row_peer(i)).wait_send()
            direct(i + 2, cell, col_peer(i)).wait_send()

    for k in range(SIDE - 1):
        for i in range(1, SIDE):
            @pl.when((row_peer(k + 1) >= PB) & (col_peer(i) >= PB))
            def _(k=k, i=i):
                half_a(k * 3 + i - 1, row_peer(k + 1), col_peer(i)).wait_send()

            @pl.when((col_peer(k + 1) >= PB) & (row_peer(i) >= PB))
            def _(k=k, i=i):
                half_b(k * 3 + i - 1, col_peer(k + 1), row_peer(i)).wait_send()


def update(panel, front):
    return pl.pallas_call(
        update_kernel,
        out_shape=jax.ShapeDtypeStruct((FRAMES, CELLS, BLK, BLK), BF16),
        in_specs=[pl.BlockSpec(memory_space=VMEM), pl.BlockSpec(memory_space=pl.ANY)],
        out_specs=pl.BlockSpec(memory_space=pl.ANY),
        scratch_shapes=[
            VMEM((CELLS, BLK, WIDTH), BF16),
            VMEM((BLK, CELLS * BLK - WIDTH), F32),
            VMEM((CELLS, BLK, BLK), BF16),
            DMA,
            DMA((6,)), DMA((CELLS,)), DMA((9,)), DMA((CELLS,)), DMA((9,)), DMA((CELLS,)),
            DMA((8, CELLS)), DMA((8, CELLS)), DMA((CELLS,)),
        ],
        compiler_params=pltpu.CompilerParams(
            collective_id=2, has_side_effects=True, vmem_limit_bytes=40 << 20
        ),
        name="update",
    )(panel, front)


GROUP = 4
SPAN = GROUP * BLK


def extend_kernel(half_ref, side_ref, parent, pieces, out, total):
    q, g = pl.program_id(0), pl.program_id(1)
    total[...] = parent[...].astype(F32)
    for c in range(FRAMES):
        half = half_ref[c]

        @pl.when(half >= 0)
        def _(c=c, half=half):
            for i in range(GROUP):
                block = q * GROUP + i

                @pl.when((block >= PB) & (side_ref[c * CELLS + block] == g))
                def _(i=i):
                    total[half, :, i * BLK:(i + 1) * BLK] += pieces[c, i].astype(F32)

    out[...] = total[...].astype(BF16)


def extend(half, side, parent, pieces):
    whole = CELLS // GROUP
    return pl.pallas_call(
        extend_kernel,
        out_shape=jax.ShapeDtypeStruct(parent.shape, BF16),
        grid_spec=pltpu.PrefetchScalarGridSpec(
            num_scalar_prefetch=2,
            grid=(whole, 2),
            in_specs=[
                pl.BlockSpec((2, BLK, SPAN), lambda q, g, h, s: (0, 0, g * whole + q)),
                pl.BlockSpec((FRAMES, GROUP, BLK, BLK), lambda q, g, h, s: (0, q, 0, 0)),
            ],
            out_specs=pl.BlockSpec((2, BLK, SPAN), lambda q, g, h, s: (0, 0, g * whole + q)),
            scratch_shapes=[VMEM((2, BLK, SPAN), F32)],
        ),
        compiler_params=pltpu.CompilerParams(vmem_limit_bytes=40 << 20),
        name="extend",
    )(half, side, parent, pieces)


def per_device(front, parent_of, block_map, parent_in):
    rows = front[0]
    cell, frame = lax.axis_index("cell"), lax.axis_index("frame")
    packed = gather_pivot(rows).reshape(BLK, PACKED)
    start = jnp.where(cell < PB, cell * BLK, WIDTH).astype(jnp.int32)[None]
    lower, panel = factor(start, packed, rows[:, :WIDTH])
    pieces = update(panel, rows)
    upper = block_map // CELLS
    mine = lax.dynamic_index_in_dim(upper, jnp.maximum(cell - PB, 0), 1, keepdims=False)
    half = jnp.where((parent_of == frame) & (cell >= PB), mine, -1).astype(jnp.int32)
    side = jnp.pad(upper, ((0, 0), (PB, 0))).reshape(-1).astype(jnp.int32)
    out = extend(half, side, parent_in[0], pieces)
    return lower[None], out[None]


def solution(mesh):
    placed = (P("frame", "cell", None), P(), P(), P("frame", None, "cell", None))
    return jax.shard_map(
        per_device,
        mesh=mesh,
        in_specs=placed,
        out_specs=(P("frame", "cell", None), P("frame", None, "cell", None)),
        check_vma=False,
    )
```

time: 606 us -> 173 us (0.29); the launches traced: 594 us -> 171 us
  other arithmetic: 238 us -> 1.36 us
  Pallas kernels: 0 us -> 161 us
  waiting for transfers between devices: 153 us -> 0 us
  local copies, waits for them, and re-layouts: 97.1 us -> 8.49 us
  matrix products: 74 us -> 0 us
  between operations: 18.5 us -> 0.68 us
  loops' own time: 14 us -> 0 us
    another operation x25 -> x0, other arithmetic: 185 us -> none  [the longest x22 124 us: per_device(): l11 = jnp.linalg.cholesky(panel[:width])]
    pallas_call x0 -> x4, Pallas kernels: none -> 161 us  [the longest x1 83 us: update(): pl.pallas_call(update_kernel, out_shape=jax.ShapeDtypeStruct((FRAMES, CEL...]
    all_gather x2 -> x0, waiting for transfers between devices: 153 us -> none  [the longest x1 101 us: per_device(): panel = lax.all_gather(block_row[:, :width], 'cell', axis=0, tiled=True)]
    another operation x21 -> x0, matrix products: 55.9 us -> none  [the longest x11 46.1 us: per_device(): lax.linalg.triangular_solve(l11, panel[width:], left_side=False, lower=Tr...]
    another operation x26 -> x0, local copies, waits for them, and re-layouts: 29.4 us -> none
    dynamic_slice x20 -> x1, local copies, waits for them, and re-layouts: 21.2 us -> 0.19 us  [per_device(): lax.dynamic_index_in_dim(upper, jnp.maximum(cell - PB, 0), 1, keepdims=Fa...]
    dynamic_update_slice x3 -> x0, other arithmetic: 19.8 us -> none  [add_piece(): return lax.dynamic_update_index_in_dim(inner, current + delta, half, 0)]
    convert_element_type x2 -> x0, other arithmetic: 18.5 us -> none  [the longest x1 9.78 us: per_device(): region_start = whole_parent[:, :, :, PB:, :].astype(jnp.float32)]
  transfers between devices with their start and end apart: 2 -> 0, of which waited for: 2 -> 0; matrix products, arithmetic and copies ran while one was open for 4% -> 0% of each run, Pallas kernels for 0% -> 0%
where the time goes in v1:
time: 173 us; the launch traced here: 171 us
  Pallas kernels  161 us (93%)
  local copies, waits for them, and re-layouts  8.49 us (5%)
    pallas_call x1, Pallas kernels, update(): pl.pallas_call(update_kernel, out_shape=jax.ShapeDtypeStruct((FRAMES, CEL...  83 us
    pallas_call x1, Pallas kernels, factor(): pl.pallas_call(factor_kernel, out_shape=(jax.ShapeDtypeStruct((BLK, WIDTH...  33.2 us
    pallas_call x1, Pallas kernels, gather_pivot(): pl.pallas_call(pivot_kernel, out_shape=jax.ShapeDtypeStruct((CELLS, PART,...  29.8 us
    pallas_call x1, Pallas kernels, extend(): pl.pallas_call(extend_kernel, out_shape=jax.ShapeDtypeStruct(parent.shape...  14.6 us
    unnamed x6, local copies, waits for them, and re-layouts  6.97 us

profile of v1, /device:TPU:15, one launch (start us, length us, event | category | flops | bytes accessed | tf_op | source)
XLA Modules:
  0.0 171.1 jit_solution(6146240940980535586)
XLA Ops:
  0.6 0.7 add_select_fusion
  1.3 0.2 dynamic-slice_reduce_fusion
  1.5 0.7 and_select_fusion.half_ref
  2.2 0.1 pad.4
  2.3 0.1 reshape.11.side_ref
  2.3 1.2 slice.4.own
  3.5 29.8 %gather_pivot.1 = f32[16,16,1536]{2,1,0:T(8,128)} custom-call(f32[256,4096]{1,0:T(8,128)} %bitcast.7), custom_call_target="tpu_custom_call" | custom-call | tf_op jit(solution)/shard_map/gather_pivot/pallas_call | solution.py:88
  33.4 0.0 copy-start.2
  33.4 1.4 copy-done.2
  34.8 33.2 %factor.1 = (f32[256,768]{1,0:T(8,128)}, bf16[256,768]{1,0:T(8,128)(2,1)S(1)}) custom-call(s32[1]{0:T(128)} %bitcast.where_ref, f32[256,1536]{1,0:T(8,128)S(1)} %bitcast.10, f32[256,768]{1,0:T(8,128)S(1)} %slice.4.own), custom_call_target="tpu_custom_call" | custom-call | tf_op jit(solution)/shard_map/factor/pallas_call | solution.py:186
  68.0 0.0 copy-start
  68.0 2.2 %copy-done = f32[1,256,4096]{2,1,0:T(8,128)S(1)} copy-done((f32[1,256,4096]{2,1,0:T(8,128)S(1)}, f32[1,256,4096]{2,1,0:T(8,128)}, u32[]{:S(2)}) %copy-start) | copy-done | bytes 4194328
  70.1 83.0 %update.1.pieces = bf16[8,16,256,256]{3,2,1,0:T(8,128)(2,1)} custom-call(bf16[256,768]{1,0:T(8,128)(2,1)S(1)} %get-tuple-element.5.panel, f32[256,4096]{1,0:T(8,128)S(1)} %bitcast.8), custom_call_target="tpu_custom_call" | custom-call | tf_op jit(solution)/shard_map/update/pallas_call | solution.py:381
  153.1 0.0 copy-start.1
  153.1 3.4 %copy-done.1 = bf16[1,2,256,8192]{3,2,1,0:T(8,128)(2,1)S(1)} copy-done((bf16[1,2,256,8192]{3,2,1,0:T(8,128)(2,1)S(1)}, bf16[1,2,256,8192]{3,2,1,0:T(8,128)(2,1)}, u32[]{:S(2)}) %copy-start.1) | copy-done | bytes 8388632
  156.5 14.6 %extend.1 = bf16[2,256,8192]{2,1,0:T(8,128)(2,1)} custom-call(s32[8]{0:T(128)S(1)} %and_select_fusion.half_ref, s32[128]{0:T(128)S(1)} %reshape.11.side_ref, bf16[2,256,8192]{2,1,0:T(8,128)(2,1)S(1)} %bitcast.9, bf16[8,16,256,256]{3,2,1,0:T(8,128)(2,1)} %update.1.pieces), custom_call_target="tpu_custom_call" | custom-call | tf_op jit(solution)/shard_map/extend/pallas_call | solution.py:425
Async XLA Ops:
  33.4 1.4 copy-start.2
  68.0 2.2 %copy-start = (f32[1,256,4096]{2,1,0:T(8,128)S(1)}, f32[1,256,4096]{2,1,0:T(8,128)}, u32[]{:S(2)}) copy-start(f32[1,256,4096]{2,1,0:T(8,128)} %param.4) | copy-start | bytes 12582916
  153.1 3.4 %copy-start.1 = (bf16[1,2,256,8192]{3,2,1,0:T(8,128)(2,1)S(1)}, bf16[1,2,256,8192]{3,2,1,0:T(8,128)(2,1)}, u32[]{:S(2)}) copy-start(bf16[1,2,256,8192]{3,2,1,0:T(8,128)(2,1)} %param.7) | copy-start | bytes 25165828

commit v2 on v0

v2 whole, which is shorter than its diff:
```python
import functools

import jax
import jax.numpy as jnp
from jax import lax
from jax.experimental import pallas as pl
from jax.experimental.pallas import tpu as pltpu
from jax.sharding import PartitionSpec as P

PB = 3
BLK = 256
F32, BF16 = jnp.float32, jnp.bfloat16
NT = (((1,), (1,)), ((), ()))
TN = (((0,), (0,)), ((), ()))
STRIP = 16
SIDE = 4
CELLS = SIDE * SIDE
FRAMES = 2 * SIDE
WIDTH = PB * BLK
VMEM = pltpu.VMEM
DMA = pltpu.SemaphoreType.DMA
MESH = pl.DeviceIdType.MESH


def remote(src, dst, send, recv, frame, cell):
    return pltpu.make_async_remote_copy(
        src_ref=src, dst_ref=dst, send_sem=send, recv_sem=recv,
        device_id=(frame, cell), device_id_type=MESH,
    )


def greet(devices):
    barrier = pltpu.get_barrier_semaphore()
    for frame, cell in devices:
        pl.semaphore_signal(barrier, inc=1, device_id=(frame, cell), device_id_type=MESH)
    pl.semaphore_wait(barrier, len(devices))


def split(x):
    hi = x.astype(BF16)
    return hi, (x - hi.astype(F32)).astype(BF16)


def dot3(a, b, dims):
    def one(u, v):
        return lax.dot_general(u, v, dims, preferred_element_type=F32)

    return one(a[0], b[0]) + one(a[0], b[1]) + one(a[1], b[0])


def strip_step(s, work, done):
    first = pl.multiple_of(s * STRIP, STRIP)
    rows = work[pl.ds(first, STRIP), :]
    left, right = rows[:, :128], rows[:, 128:]
    turned = pltpu.roll(left, lax.rem(128 - first, 128), 1)
    cols = [jnp.broadcast_to(turned[:, b:b + 1], (STRIP, 128)) for b in range(STRIP)]
    row_no = lax.broadcasted_iota(jnp.int32, (STRIP, 128), 0)
    lane = lax.broadcasted_iota(jnp.int32, (STRIP, 128), 1)
    scale = jnp.zeros((STRIP, 128), F32)
    for a in range(STRIP):
        below = jnp.where(row_no > a, cols[a], 0.0)
        root = jnp.broadcast_to(lax.rsqrt(cols[a][a:a + 1, :]), (STRIP, 128))
        over = root * root
        scale = jnp.where(row_no == a, root, scale)
        if a < STRIP - 1:
            for b in range(a + 1, STRIP):
                cols[b] = cols[b] - (below * cols[b][a:a + 1, :]) * over
            ratio = below * over
            left = left - ratio * left[a:a + 1, :]
            right = right - ratio * right[a:a + 1, :]
    upper = jnp.where(lane >= row_no + first, left * scale, 0.0)
    inverse = right * scale
    done[pl.ds(first, STRIP), :128] = upper
    done[pl.ds(first, STRIP), 128:] = inverse
    u1, u2 = split(upper)
    v1, v2 = split(inverse)
    one, two = jnp.concatenate([u1, v1], 1), jnp.concatenate([u2, v2], 1)
    work[...] -= lax.dot_general(
        jnp.concatenate([u1, u1, u2], 0), jnp.concatenate([one, two, one], 0), TN,
        preferred_element_type=F32,
    )


LAG, LAG2, STEPS = 2, 4, CELLS
HALF = BLK // 2
ORDER = (1, 3, 2)


def fronts_kernel(
    front, lower, pieces,
    raw, a, a_hi, a_lo, own, own_hi, own_lo, inv_hi, inv_lo, work, done,
    stage_a, stage_b, held, rest, chunk,
    load_sem, s1_send, s1_recv, s1_keep, s2_send, s2_recv,
    d_send, d_recv, f_send, f_recv, l_send, l_recv, h_send, h_recv,
    x_send, x_recv, keep_sem,
):
    frame, cell = lax.axis_index("frame"), lax.axis_index("cell")
    x, core = frame // 2, lax.rem(frame, 2)
    y, z = cell // SIDE, lax.rem(cell, SIDE)
    right = lax.rem(x + 1, SIDE) * 2 + core
    left = lax.rem(x + SIDE - 1, SIDE) * 2 + core
    across = lax.rem(x + 2, SIDE) * 2 + core
    sibling = x * 2 + 1 - core
    has_rows = cell >= PB

    def row_peer(i):
        return y * SIDE + lax.rem(z + i, SIDE)

    def col_peer(i):
        return lax.rem(y + i, SIDE) * SIDE + z

    load_own = pltpu.make_async_copy(front.at[:, pl.ds(0, WIDTH)], own, load_sem.at[0])
    load_rest = pltpu.make_async_copy(
        front.at[:, pl.ds(WIDTH, CELLS * BLK - WIDTH)], rest, load_sem.at[1]
    )
    greet(
        [(frame, row_peer(i)) for i in range(1, SIDE)]
        + [(frame, col_peer(i)) for i in range(1, SIDE)]
        + [(left, cell), (right, cell), (sibling, cell)]
    )

    def stage_copy(r, kind, i):
        wide = pl.ds(0, BLK * (r + 1))
        if kind == 0:
            to, first, buffer = lax.rem(r + i, SIDE), 32 * ((r + i) % SIDE), stage_a
        else:
            to, first, buffer = i * SIDE + r, HALF + 32 * i, stage_b
        src, dst = front.at[pl.ds(first, 32), wide], buffer.at[r, :, wide]
        if i == 0:
            return pltpu.make_async_copy(src, dst, s1_keep.at[kind])
        return remote(src, dst, s1_send.at[kind, i], s1_recv.at[kind, r], frame, to)

    def region(r, kind, ys, zs):
        if kind == 0:
            first = BLK * r + 32 * zs + 8 * ys
        else:
            first = BLK * r + HALF + 32 * ys + 8 * zs
        return raw.at[pl.ds(pl.multiple_of(first, 8), 8), pl.ds(0, BLK * (r + 1))]

    def part_copy(r, kind, i):
        wide = pl.ds(0, BLK * (r + 1))
        if kind == 0:
            at = lax.rem(y + i, SIDE)
            to, dst, buffer = col_peer(i), region(r, 0, at, z), stage_a
        else:
            at = lax.rem(z + i, SIDE)
            to, dst, buffer = row_peer(i), region(r, 1, y, at), stage_b
        src = buffer.at[r, pl.ds(pl.multiple_of(8 * at, 8), 8), wide]
        if i == 0:
            return src, dst
        return remote(src, dst, s2_send.at[r, kind, i], s2_recv.at[r, kind], frame, to)

    def to_peer(r, kind, slot, to):
        part = region(r, kind, y, z)
        return remote(part, part, d_send.at[r, kind, slot], d_recv.at[r, kind, cell], frame, to)

    def from_peer(r, kind, ys, zs):
        part, src = region(r, kind, ys, zs), ys * SIDE + zs
        remote(part, part, d_send.at[r, kind, 0], d_recv.at[r, kind, src], frame, src).wait_recv()

    def forward(r, kind, slot, ys, zs, to):
        part, src = region(r, kind, ys, zs), ys * SIDE + zs
        return remote(part, part, f_send.at[r, kind, slot], f_recv.at[r, kind, src], frame, to)

    def pivot_start():
        for r in range(PB):
            @pl.when(cell == r)
            def _(r=r):
                for i in (0,) + ORDER:
                    for kind in range(2):
                        stage_copy(r, kind, i).start()

    def pivot_parts(r):
        for kind, holds in ((0, y == 0), (1, z == r)):
            @pl.when(holds)
            def _(kind=kind):
                @pl.when(cell == r)
                def _():
                    stage_copy(r, kind, 0).wait()

                @pl.when(cell != r)
                def _():
                    stage_copy(r, kind, 1).wait_recv()

                for i in ORDER:
                    part_copy(r, kind, i).start()
                src, dst = part_copy(r, kind, 0)
                dst[...] = src[...]

            @pl.when(jnp.logical_not(holds))
            def _(kind=kind):
                part = region(r, kind, y, z)
                remote(part, part, s2_send.at[r, kind, 0], s2_recv.at[r, kind], frame, cell).wait_recv()

        for i in ORDER:
            for kind in range(2):
                to_peer(r, kind, i - 1, row_peer(i)).start()
                to_peer(r, kind, i + 2, col_peer(i)).start()

    def pivot_forward(r):
        for i in ORDER:
            zs, ys = lax.rem(z + i, SIDE), lax.rem(y + i, SIDE)
            from_peer(r, 0, y, zs)
            for k in ORDER:
                forward(r, 0, (i - 1) * 3 + k - 1, y, zs, col_peer(k)).start()
            from_peer(r, 1, ys, z)
            for k in ORDER:
                forward(r, 1, (i - 1) * 3 + k - 1, ys, z, row_peer(k)).start()
        for i in ORDER:
            from_peer(r, 1, y, lax.rem(z + i, SIDE))
            from_peer(r, 0, lax.rem(y + i, SIDE), z)

    def pivot_end(r):
        for i in ORDER:
            for k in ORDER:
                ys, zs = lax.rem(y + i, SIDE), lax.rem(z + k, SIDE)
                for kind in range(2):
                    forward(r, kind, 0, ys, zs, cell).wait_recv()

    def pivot_sent(r):
        @pl.when(cell == r)
        def _():
            for i in ORDER:
                for kind in range(2):
                    stage_copy(r, kind, i).wait_send()

        for kind, holds in ((0, y == 0), (1, z == r)):
            @pl.when(holds)
            def _(kind=kind):
                for i in ORDER:
                    part_copy(r, kind, i).wait_send()

            for i in ORDER:
                to_peer(r, kind, i - 1, row_peer(i)).wait_send()
                to_peer(r, kind, i + 2, col_peer(i)).wait_send()
                for k in ORDER:
                    slot = (i - 1) * 3 + k - 1
                    if kind == 0:
                        forward(r, 0, slot, y, lax.rem(z + i, SIDE), col_peer(k)).wait_send()
                    else:
                        forward(r, 1, slot, lax.rem(y + i, SIDE), z, row_peer(k)).wait_send()

    def panel_step(source, full, hi, lo, first, count, j):
        rows, here = pl.ds(first, count), pl.ds(128 * j, 128)
        value = source[rows, here]
        if j > 0:
            past = pl.ds(0, 128 * j)
            value = value - dot3((hi[rows, past], lo[rows, past]), (a_hi[here, past], a_lo[here, past]), NT)
        value = dot3(split(value), (inv_hi[j], inv_lo[j]), NT)
        full[rows, here] = value
        hi[rows, here], lo[rows, here] = split(value)

    def pivot_step(j):
        here, past = pl.ds(128 * j, 128), pl.ds(0, 128 * j)
        value = raw[here, here]
        if j > 0:
            both = a_hi[here, past], a_lo[here, past]
            value = value - dot3(both, both, NT)
        work[:, :128] = value
        work[:, 128:] = (
            lax.broadcasted_iota(jnp.int32, (128, 128), 0)
            == lax.broadcasted_iota(jnp.int32, (128, 128), 1)
        ).astype(F32)

        def step(s, carry):
            strip_step(s, work, done)
            return carry

        lax.fori_loop(0, 128 // STRIP, step, 0)
        inv_hi[j], inv_lo[j] = split(done[:, 128:])
        a[here, here] = done[:, :128].T

    def panel_to(q, slot, to):
        block = held.at[q, cell]
        return remote(block, block, l_send.at[q, slot], l_recv.at[q, cell], frame, to)

    def half_block(q, kind, src):
        return held.at[q, src, pl.ds(HALF * kind, HALF)]

    def half_to(q, kind, slot, src, to):
        block = half_block(q, kind, src)
        return remote(block, block, h_send.at[q, kind, slot], h_recv.at[q, kind, src], frame, to)

    def own_step(q):
        @pl.when(has_rows)
        def _():
            panel_step(own, own, own_hi, own_lo, 0, BLK, 2 * q)
            panel_step(own, own, own_hi, own_lo, 0, BLK, 2 * q + 1)
            held[q, cell] = own_hi[:, BLK * q:BLK * (q + 1)]
            for i in ORDER:
                panel_to(q, i - 1, row_peer(i)).start()
                panel_to(q, i + 2, col_peer(i)).start()

    def panel_forward(q, i, by_row, act):
        src = row_peer(i) if by_row else col_peer(i)

        @pl.when(src >= PB)
        def _():
            if act == "start":
                block = held.at[q, src]
                remote(block, block, l_send.at[q, 0], l_recv.at[q, src], frame, src).wait_recv()
            for k in ORDER:
                to = col_peer(k) if by_row else row_peer(k)

                @pl.when(to >= PB)
                def _(to=to, k=k):
                    copy = half_to(q, 0 if by_row else 1, (i - 1) * 3 + k - 1, src, to)
                    copy.start() if act == "start" else copy.wait_send()

    pivot_start()
    load_own.start()

    @pl.when(has_rows)
    def _():
        load_rest.start()

    pivot_parts(0)
    pivot_forward(0)
    pivot_parts(1)
    pivot_end(0)
    load_own.wait()
    pivot_step(0)
    pivot_forward(1)
    panel_step(raw, a, a_hi, a_lo, 128, 128, 0)
    pivot_step(1)
    pivot_parts(2)
    own_step(0)
    pivot_end(1)
    for j in range(2):
        panel_step(raw, a, a_hi, a_lo, BLK, BLK, j)
    pivot_step(2)
    pivot_forward(2)
    panel_step(raw, a, a_hi, a_lo, 384, 128, 2)
    pivot_step(3)
    own_step(1)
    for i in ORDER:
        panel_forward(0, i, True, "start")
        panel_forward(0, i, False, "start")
    pivot_end(2)
    for j in range(4):
        panel_step(raw, a, a_hi, a_lo, 2 * BLK, BLK, j)
    pivot_step(4)
    panel_step(raw, a, a_hi, a_lo, 640, 128, 4)
    pivot_step(5)
    own_step(2)
    for i in ORDER:
        panel_forward(1, i, True, "start")
        panel_forward(1, i, False, "start")

    def order(t):
        pair, by_row = (t - 1) // 2, lax.rem(t - 1, 2) == 0
        i = jnp.where(pair == 0, 1, jnp.where(pair == 1, 3, 2))
        u = t - 7
        dy = jnp.where(t == 0, 0, jnp.where(t < 7, jnp.where(by_row, 0, i), 1 + u // 3))
        dz = jnp.where(t == 0, 0, jnp.where(t < 7, jnp.where(by_row, i, 0), 1 + lax.rem(u, 3)))
        return lax.rem(y + dy, SIDE) * SIDE + lax.rem(z + dz, SIDE)

    whole = pl.ds(0, BLK)

    def x_copy(kind, c):
        source, rows, to = [
            (frame, whole, right), (frame, whole, left), (frame, whole, sibling),
            (left, pl.ds(0, HALF), right), (left, whole, sibling),
            (right, pl.ds(HALF, HALF), left), (right, whole, sibling),
            (across, whole, sibling),
        ][kind]
        dst = pieces.at[source, c, rows]
        src = chunk.at[c, rows] if kind < 3 else dst
        return remote(src, dst, x_send.at[kind, c], x_recv.at[kind, c], to, cell)

    def arrived(kind, source, rows, c):
        dst = pieces.at[source, c, rows]
        remote(dst, dst, x_send.at[kind, c], x_recv.at[kind, c], sibling, cell).wait_recv()

    def keep(c):
        return pltpu.make_async_copy(chunk.at[c], pieces.at[frame, c], keep_sem.at[c])

    def step(t, carry):
        c = order(t)
        for n, i in enumerate(ORDER):
            for by_row in (True, False):
                @pl.when(t == 1 + 2 * n + (0 if by_row else 1))
                def _(i=i, by_row=by_row):
                    panel_forward(2, i, by_row, "start")

        @pl.when((t < STEPS) & (c >= PB) & has_rows)
        def _():
            @pl.when(t == 0)
            def _():
                load_rest.wait()

            @pl.when(t >= 7)
            def _():
                for q in range(PB):
                    for kind in range(2):
                        half_to(q, kind, 0, c, cell).wait_recv()

            value = rest[:, pl.ds(pl.multiple_of((c - PB) * BLK, BLK), BLK)]
            for q in range(PB):
                value = value - lax.dot_general(
                    own_hi[:, BLK * q:BLK * (q + 1)], held[q, c], NT, preferred_element_type=F32
                )
            chunk[c] = value.astype(BF16)
            keep(c).start()
            for kind in range(3):
                x_copy(kind, c).start()

        back = order(t - LAG)

        @pl.when((t >= LAG) & (t < STEPS + LAG) & has_rows & (back >= PB))
        def _():
            arrived(0, left, whole, back)
            x_copy(3, back).start()
            x_copy(4, back).start()
            arrived(1, right, whole, back)
            x_copy(5, back).start()
            x_copy(6, back).start()

        far = order(t - LAG2)

        @pl.when((t >= LAG2) & has_rows & (far >= PB))
        def _():
            arrived(3, across, pl.ds(0, HALF), far)
            arrived(5, across, pl.ds(HALF, HALF), far)
            x_copy(7, far).start()

        return carry

    lax.fori_loop(0, STEPS + LAG2, step, 0)

    for r in range(PB):
        @pl.when(cell == r)
        def _(r=r):
            row_no = lax.broadcasted_iota(jnp.int32, (BLK, WIDTH), 0) + BLK * r
            col_no = lax.broadcasted_iota(jnp.int32, (BLK, WIDTH), 1)
            lower[...] = jnp.where(row_no >= col_no, a[BLK * r:BLK * (r + 1), :], 0.0)

    @pl.when(has_rows)
    def _():
        lower[...] = own[...]

    def finish(t, carry):
        @pl.when(has_rows & (t >= PB))
        def _():
            other = 1 - 2 * core
            arrived(2, sibling, whole, t)
            arrived(4, left + other, whole, t)
            arrived(6, right + other, whole, t)
            arrived(7, across + other, whole, t)
            keep(t).wait()
            for kind in range(8):
                x_copy(kind, t).wait_send()

        return carry

    for r in range(PB):
        pivot_sent(r)
    for q in range(PB):
        @pl.when(has_rows)
        def _(q=q):
            for i in ORDER:
                panel_to(q, i - 1, row_peer(i)).wait_send()
                panel_to(q, i + 2, col_peer(i)).wait_send()

        for i in ORDER:
            panel_forward(q, i, True, "end")
            panel_forward(q, i, False, "end")
    lax.fori_loop(0, CELLS, finish, 0)


def fronts(front):
    rest = CELLS * BLK - WIDTH
    return pl.pallas_call(
        fronts_kernel,
        out_shape=(
            jax.ShapeDtypeStruct((BLK, WIDTH), F32),
            jax.ShapeDtypeStruct((FRAMES, CELLS, BLK, BLK), BF16),
        ),
        in_specs=[pl.BlockSpec(memory_space=pl.ANY)],
        out_specs=(pl.BlockSpec(memory_space=VMEM), pl.BlockSpec(memory_space=pl.ANY)),
        scratch_shapes=[
            VMEM((WIDTH, WIDTH), F32), VMEM((WIDTH, WIDTH), F32),
            VMEM((WIDTH, WIDTH), BF16), VMEM((WIDTH, WIDTH), BF16),
            VMEM((BLK, WIDTH), F32), VMEM((BLK, WIDTH), BF16), VMEM((BLK, WIDTH), BF16),
            VMEM((WIDTH // 128, 128, 128), BF16), VMEM((WIDTH // 128, 128, 128), BF16),
            VMEM((128, 256), F32), VMEM((128, 256), F32),
            VMEM((PB, 32, WIDTH), F32), VMEM((PB, 32, WIDTH), F32),
            VMEM((PB, CELLS, BLK, BLK), BF16), VMEM((BLK, rest), F32), VMEM((CELLS, BLK, BLK), BF16),
            DMA((2,)), DMA((2, SIDE)), DMA((2, PB)), DMA((2,)), DMA((PB, 2, SIDE)), DMA((PB, 2)),
            DMA((PB, 2, 6)), DMA((PB, 2, CELLS)), DMA((PB, 2, 9)), DMA((PB, 2, CELLS)),
            DMA((PB, 6)), DMA((PB, CELLS)), DMA((PB, 2, 9)), DMA((PB, 2, CELLS)),
            DMA((8, CELLS)), DMA((8, CELLS)), DMA((CELLS,)),
        ],
        compiler_params=pltpu.CompilerParams(
            collective_id=1, has_side_effects=True, vmem_limit_bytes=56 << 20
        ),
        name="fronts",
    )(front)


GROUP = 4
SPAN = GROUP * BLK
WHOLE = CELLS // GROUP


def extend_kernel(parent_of, block_map, parent, pieces, out, total, buffer, sems):
    q, g = pl.program_id(0), pl.program_id(1)
    frame, cell = lax.axis_index("frame"), lax.axis_index("cell")
    turn = lax.rem(q, 2)

    def live(c):
        return (parent_of[c] == frame) & (cell >= PB)

    def fetch(c, at):
        slot = lax.rem(at, 2)
        return pltpu.make_async_copy(
            pieces.at[c, pl.ds(at * GROUP, GROUP)], buffer.at[slot, c], sems.at[slot, c]
        )

    for c in range(FRAMES):
        @pl.when(live(c) & (q == 0) & (g == 0))
        def _(c=c):
            fetch(c, q).start()

    for c in range(FRAMES):
        @pl.when(live(c) & (q + 1 < WHOLE) & (g == 0))
        def _(c=c):
            fetch(c, q + 1).start()

    total[...] = parent[...].astype(F32)
    for c in range(FRAMES):
        @pl.when(live(c))
        def _(c=c):
            half = block_map[c, jnp.maximum(cell - PB, 0)] // CELLS

            @pl.when(g == 0)
            def _():
                fetch(c, q).wait()

            for i in range(GROUP):
                block = q * GROUP + i

                @pl.when((block >= PB) & (block_map[c, jnp.maximum(block - PB, 0)] // CELLS == g))
                def _(i=i):
                    total[half, :, i * BLK:(i + 1) * BLK] += buffer[turn, c, i].astype(F32)

    out[...] = total[...].astype(BF16)


def extend(parent_of, block_map, parent, pieces):
    tile = pl.BlockSpec((2, BLK, SPAN), lambda q, g, *_: (0, 0, g * WHOLE + q))
    return pl.pallas_call(
        extend_kernel,
        out_shape=jax.ShapeDtypeStruct(parent.shape, BF16),
        grid_spec=pltpu.PrefetchScalarGridSpec(
            num_scalar_prefetch=2,
            grid=(WHOLE, 2),
            in_specs=[tile, pl.BlockSpec(memory_space=pl.ANY)],
            out_specs=tile,
            scratch_shapes=[
                VMEM((2, BLK, SPAN), F32), VMEM((2, FRAMES, GROUP, BLK, BLK), BF16), DMA((2, FRAMES)),
            ],
        ),
        compiler_params=pltpu.CompilerParams(vmem_limit_bytes=60 << 20),
        name="extend",
    )(parent_of, block_map, parent, pieces)


def per_device(front, parent_of, block_map, parent_in):
    lower, pieces = fronts(front[0])
    out = extend(parent_of, block_map, parent_in[0], pieces)
    return lower[None], out[None]


def solution(mesh):
    placed = (P("frame", "cell", None), P(), P(), P("frame", None, "cell", None))
    return jax.shard_map(
        per_device,
        mesh=mesh,
        in_specs=placed,
        out_specs=(P("frame", "cell", None), P("frame", None, "cell", None)),
        check_vma=False,
    )
```

time: 606 us -> 148 us (0.24); the launches traced: 594 us -> 146 us
  other arithmetic: 238 us -> 0 us
  waiting for transfers between devices: 153 us -> 0 us
  Pallas kernels: 0 us -> 145 us
  local copies, waits for them, and re-layouts: 97.1 us -> 0.89 us
  matrix products: 74 us -> 0 us
  between operations: 18.5 us -> 0.66 us
  loops' own time: 14 us -> 0 us
    another operation x25 -> x0, other arithmetic: 185 us -> none  [the longest x22 124 us: per_device(): l11 = jnp.linalg.cholesky(panel[:width])]
    all_gather x2 -> x0, waiting for transfers between devices: 153 us -> none  [the longest x1 101 us: per_device(): panel = lax.all_gather(block_row[:, :width], 'cell', axis=0, tiled=True)]
    pallas_call x0 -> x2, Pallas kernels: none -> 145 us  [the longest x1 133 us: fronts(): pl.pallas_call(fronts_kernel, out_shape=(jax.ShapeDtypeStruct((BLK, WIDTH...]
    another operation x21 -> x0, matrix products: 55.9 us -> none  [the longest x11 46.1 us: per_device(): lax.linalg.triangular_solve(l11, panel[width:], left_side=False, lower=Tr...]
    another operation x26 -> x0, local copies, waits for them, and re-layouts: 29.4 us -> none
    unnamed x20 -> x3, local copies, waits for them, and re-layouts: 24.3 us -> 0.89 us
    dynamic_slice x20 -> x0, local copies, waits for them, and re-layouts: 21.2 us -> none  [the longest x8 10.7 us: one_child(): target = lax.dynamic_index_in_dim(positions, which_k, 0, keepdims=False)]
    dynamic_update_slice x3 -> x0, other arithmetic: 19.8 us -> none  [add_piece(): return lax.dynamic_update_index_in_dim(inner, current + delta, half, 0)]
  transfers between devices with their start and end apart: 2 -> 0, of which waited for: 2 -> 0; matrix products, arithmetic and copies ran while one was open for 4% -> 0% of each run, Pallas kernels for 0% -> 0%
where the time goes in v2:
time: 148 us; the launch traced here: 146 us
  Pallas kernels  145 us (98%)
    pallas_call x1, Pallas kernels, fronts(): pl.pallas_call(fronts_kernel, out_shape=(jax.ShapeDtypeStruct((BLK, WIDTH...  133 us
    pallas_call x1, Pallas kernels, extend(): pl.pallas_call(extend_kernel, out_shape=jax.ShapeDtypeStruct(parent.shape...  12.3 us

profile of v2, /device:TPU:15, one launch (start us, length us, event | category | flops | bytes accessed | tf_op | source)
XLA Modules:
  0.0 146.4 jit_solution(14979106895593318176)
XLA Ops:
  0.6 132.6 %fronts.1 = (f32[256,768]{1,0:T(8,128)}, bf16[8,16,256,256]{3,2,1,0:T(8,128)(2,1)}) custom-call(f32[256,4096]{1,0:T(8,128)} %bitcast.6), custom_call_target="tpu_custom_call" | custom-call | tf_op jit(solution)/shard_map/fronts/pallas_call | solution.py:473
  133.2 0.0 copy-start
  133.3 12.3 %extend.1 = bf16[2,256,8192]{2,1,0:T(8,128)(2,1)} custom-call(s32[8]{0:T(128)} %parent_of.1, s32[8,13]{1,0:T(8,128)} %block_map.1, bf16[2,256,8192]{2,1,0:T(8,128)(2,1)} %bitcast.4, bf16[8,16,256,256]{3,2,1,0:T(8,128)(2,1)} %get-tuple-element.5.pieces), custom_call_target="tpu_custom_call" | custom-call | tf_op jit(solution)/shard_map/extend/pallas_call | solution.py:552
  145.6 0.0 copy-done
  145.6 0.9 copy.7
Async XLA Ops:
  133.2 12.3 %copy-start = (f32[256,768]{1,0:T(8,128)S(1)}, f32[256,768]{1,0:T(8,128)}, u32[]{:S(2)}) copy-start(f32[256,768]{1,0:T(8,128)} %get-tuple-element.4) | copy-start | bytes 2359300

commit v3 on v2

v3 whole, which is shorter than its diff:
```python
import functools

import jax
import jax.numpy as jnp
from jax import lax
from jax.experimental import pallas as pl
from jax.experimental.pallas import tpu as pltpu
from jax.sharding import PartitionSpec as P

PB = 3
BLK = 256
F32, BF16 = jnp.float32, jnp.bfloat16
NT = (((1,), (1,)), ((), ()))
TN = (((0,), (0,)), ((), ()))
STRIP = 16
SIDE = 4
CELLS = SIDE * SIDE
FRAMES = 2 * SIDE
WIDTH = PB * BLK
VMEM = pltpu.VMEM
DMA = pltpu.SemaphoreType.DMA
MESH = pl.DeviceIdType.MESH


def remote(src, dst, send, recv, frame, cell):
    return pltpu.make_async_remote_copy(
        src_ref=src, dst_ref=dst, send_sem=send, recv_sem=recv,
        device_id=(frame, cell), device_id_type=MESH,
    )


def greet(devices):
    barrier = pltpu.get_barrier_semaphore()
    for frame, cell in devices:
        pl.semaphore_signal(barrier, inc=1, device_id=(frame, cell), device_id_type=MESH)
    pl.semaphore_wait(barrier, len(devices))


def split(x):
    hi = x.astype(BF16)
    return hi, (x - hi.astype(F32)).astype(BF16)


def dot3(a, b, dims):
    def one(u, v):
        return lax.dot_general(u, v, dims, preferred_element_type=F32)

    return one(a[0], b[0]) + one(a[0], b[1]) + one(a[1], b[0])


def strip_static(s, work, done):
    first = STRIP * s
    left_t, left_b = work[first:first + 8, :128], work[first + 8:first + 16, :128]
    right_t, right_b = work[first:first + 8, 128:], work[first + 8:first + 16, 128:]
    spread = lambda v, b: jnp.broadcast_to(v[:, first + b:first + b + 1], (8, 128))
    pick = lambda v, a: jnp.broadcast_to(v[a:a + 1, :], (8, 128))
    cols_t = [spread(left_t, b) for b in range(STRIP)]
    cols_b = [spread(left_b, b) for b in range(STRIP)]
    row_no = lax.broadcasted_iota(jnp.int32, (8, 128), 0)
    lane = lax.broadcasted_iota(jnp.int32, (8, 128), 1)
    scale_t = scale_b = jnp.zeros((8, 128), F32)
    for a in range(8):
        root = lax.rsqrt(pick(cols_t[a], a))
        over = root * root
        scale_t = jnp.where(row_no == a, root, scale_t)
        ratio_t = jnp.where(row_no > a, cols_t[a], 0.0) * over
        ratio_b = cols_b[a] * over
        for b in range(a + 1, STRIP):
            here = pick(cols_t[b], a)
            if a < 7:
                cols_t[b] = cols_t[b] - ratio_t * here
            cols_b[b] = cols_b[b] - ratio_b * here
        l, r = pick(left_t, a), pick(right_t, a)
        left_t, right_t = left_t - ratio_t * l, right_t - ratio_t * r
        left_b, right_b = left_b - ratio_b * l, right_b - ratio_b * r
    for a in range(8):
        root = lax.rsqrt(pick(cols_b[8 + a], a))
        scale_b = jnp.where(row_no == a, root, scale_b)
        if a == 7:
            break
        ratio_b = jnp.where(row_no > a, cols_b[8 + a], 0.0) * (root * root)
        for b in range(9 + a, STRIP):
            cols_b[b] = cols_b[b] - ratio_b * pick(cols_b[b], a)
        l, r = pick(left_b, a), pick(right_b, a)
        left_b, right_b = left_b - ratio_b * l, right_b - ratio_b * r
    up = jnp.concatenate([
        jnp.where(lane >= row_no + first, left_t * scale_t, 0.0),
        jnp.where(lane >= row_no + first + 8, left_b * scale_b, 0.0)], 0)
    inv = jnp.concatenate([right_t * scale_t, right_b * scale_b], 0)
    done[first:first + STRIP, :128] = up
    done[first:first + STRIP, 128:] = inv
    end = first + STRIP
    if end < 128:
        u1, u2 = split(up)
        v1, v2 = split(inv)
        lhs = jnp.concatenate([u1, u1, u2], 0)
        one, two = jnp.concatenate([u1, v1], 1), jnp.concatenate([u2, v2], 1)
        rhs = jnp.concatenate([one, two, one], 0)
        work[end:, :] -= lax.dot_general(lhs, rhs, TN, preferred_element_type=F32)[end:]


LAG, LAG2, STEPS = 5, 10, CELLS
HALF = BLK // 2
ORDER = (1, 3, 2)
PANELS = ((0, 256), (256, 256), (512, 128), (640, 128))


def fronts_kernel(
    front, lower, pieces,
    raw, a, a_hi, a_lo, own, own_hi, own_lo, inv_hi, inv_lo, work, done,
    held, rest, chunk,
    load_sem, s1_send, s1_recv, s1_keep, s2_send, s2_recv, s3_send, s3_recv,
    l_send, l_recv, h_send, h_recv,
    x_send, near, far_sem, late, keep_sem,
):
    frame, cell = lax.axis_index("frame"), lax.axis_index("cell")
    x, core = frame // 2, lax.rem(frame, 2)
    y, z = cell // SIDE, lax.rem(cell, SIDE)
    right = lax.rem(x + 1, SIDE) * 2 + core
    left = lax.rem(x + SIDE - 1, SIDE) * 2 + core
    across = lax.rem(x + 2, SIDE) * 2 + core
    sibling = x * 2 + 1 - core
    has_rows = cell >= PB

    def row_peer(i):
        return y * SIDE + lax.rem(z + i, SIDE)

    def col_peer(i):
        return lax.rem(y + i, SIDE) * SIDE + z

    load_own = pltpu.make_async_copy(front.at[:, pl.ds(0, WIDTH)], own, load_sem.at[0])
    load_rest = pltpu.make_async_copy(
        front.at[:, pl.ds(WIDTH, CELLS * BLK - WIDTH)], rest, load_sem.at[1]
    )
    greet(
        [(frame, row_peer(i)) for i in range(1, SIDE)]
        + [(frame, col_peer(i)) for i in range(1, SIDE)]
        + [(left, cell), (right, cell), (sibling, cell)]
    )

    def quarter(r, kind, at):
        first = pl.multiple_of(BLK * r + HALF * kind + 32 * at, 32)
        return raw.at[pl.ds(first, 32), pl.ds(0, BLK * r + 128 * (kind + 1))]

    def place(kind):
        return z if kind == 0 else y

    def along(kind, i):
        return row_peer(i) if kind == 0 else col_peer(i)

    def first_copy(r, kind, i):
        at = (r + i) % SIDE if kind == 0 else i
        src = front.at[pl.ds(HALF * kind + 32 * at, 32), pl.ds(0, BLK * r + 128 * (kind + 1))]
        if i == 0:
            return pltpu.make_async_copy(src, quarter(r, kind, at), s1_keep.at[kind])
        return remote(
            src, quarter(r, kind, at), s1_send.at[0], s1_recv.at[kind, r], frame,
            at if kind == 0 else at * SIDE + r,
        )

    def second_copy(r, kind, i):
        part = quarter(r, kind, place(kind))
        return remote(part, part, s2_send.at[r, kind], s2_recv.at[r, kind], frame, along(1 - kind, i))

    def third_copy(r, kind, i):
        part = quarter(r, kind, place(kind))
        return remote(
            part, part, s3_send.at[r, kind], s3_recv.at[r], frame, along(kind, i)
        )

    def pivot_start():
        for r in range(PB):
            @pl.when(cell == r)
            def _(r=r):
                for i in (0,) + ORDER:
                    for kind in range(2):
                        first_copy(r, kind, i).start()

    def pivot_send(r):
        for kind, holds in ((0, y == 0), (1, z == r)):
            @pl.when(holds)
            def _(kind=kind):
                @pl.when(cell == r)
                def _():
                    first_copy(r, kind, 0).wait()

                @pl.when(cell != r)
                def _():
                    part = quarter(r, kind, place(kind))
                    remote(part, part, s1_send.at[0], s1_recv.at[kind, r], frame, cell).wait_recv()

                for i in ORDER:
                    second_copy(r, kind, i).start()

            @pl.when(jnp.logical_not(holds))
            def _(kind=kind):
                second_copy(r, kind, 0).wait_recv()

            for i in ORDER:
                third_copy(r, kind, i).start()

    def six(r):
        return raw.at[pl.ds(0, 32 * (4 * r + 3)), pl.ds(0, 384)]

    def pivot_end(r):
        part = six(r)
        remote(part, part, s3_send.at[r, 0], s3_recv.at[r], frame, cell).wait_recv()

    def pivot_sent(r):
        @pl.when(cell == r)
        def _():
            part = six(r)
            remote(part, part, s1_send.at[0], s1_recv.at[0, r], frame, cell).wait_send()

        for kind, holds in ((0, y == 0), (1, z == r)):
            part = raw.at[pl.ds(0, 3 * 32), pl.ds(0, BLK * r + 128 * (kind + 1))]

            @pl.when(holds)
            def _(kind=kind, part=part):
                remote(part, part, s2_send.at[r, kind], s2_recv.at[r, kind], frame, cell).wait_send()

            remote(part, part, s3_send.at[r, kind], s3_recv.at[r], frame, cell).wait_send()

    def panel_step(source, full, hi, lo, first, count, j):
        rows, here = pl.ds(first, count), pl.ds(128 * j, 128)
        value = source[rows, here]
        if j > 0:
            past = pl.ds(0, 128 * j)
            value = value - dot3((hi[rows, past], lo[rows, past]), (a_hi[here, past], a_lo[here, past]), NT)
        value = dot3(split(value), (inv_hi[j], inv_lo[j]), NT)
        full[rows, here] = value
        hi[rows, here], lo[rows, here] = split(value)

    def pivot_step(j):
        here, past = pl.ds(128 * j, 128), pl.ds(0, 128 * j)
        value = raw[here, here]
        if j > 0:
            both = a_hi[here, past], a_lo[here, past]
            value = value - dot3(both, both, NT)
        work[:, :128] = value
        work[:, 128:] = (
            lax.broadcasted_iota(jnp.int32, (128, 128), 0)
            == lax.broadcasted_iota(jnp.int32, (128, 128), 1)
        ).astype(F32)

        for s in range(128 // STRIP):
            strip_static(s, work, done)
        inv_hi[j], inv_lo[j] = split(done[:, 128:])
        a[here, here] = done[:, :128].T

    def block(q, src, first, count):
        start, wide = PANELS[q]
        return held.at[start // BLK, src, pl.ds(first, count), pl.ds(start % BLK, wide)]

    def panel_to(q, i, by_row):
        to, slot = (row_peer(i), 3 - i) if by_row else (col_peer(i), 6 - i)
        part = block(q, cell, 0, BLK)
        return remote(part, part, l_send.at[q], l_recv.at[q, slot], frame, to)

    def half_to(q, kind, src, to):
        part = block(q, src, HALF * kind, HALF)
        return remote(part, part, h_send.at[q, kind], h_recv.at[src], frame, to)

    def own_step(q):
        start, wide = PANELS[q]

        @pl.when(has_rows)
        def _():
            for j in range(start // 128, (start + wide) // 128):
                panel_step(own, own, own_hi, own_lo, 0, BLK, j)
            here = pl.ds(start % BLK, wide)
            held[start // BLK, cell, :, here] = own_hi[:, start:start + wide]
            for i in ORDER:
                panel_to(q, i, True).start()
                panel_to(q, i, False).start()

    def panel_forward(q, i, by_row):
        src, slot = (row_peer(i), i - 1) if by_row else (col_peer(i), i + 2)

        @pl.when(src >= PB)
        def _():
            part = block(q, src, 0, BLK)
            remote(part, part, l_send.at[q], l_recv.at[q, slot], frame, src).wait_recv()
            for k in ORDER:
                to = col_peer(k) if by_row else row_peer(k)

                @pl.when(to >= PB)
                def _(to=to):
                    half_to(q, 0 if by_row else 1, src, to).start()

    def forward_all(q):
        for i in ORDER:
            panel_forward(q, i, True)
            panel_forward(q, i, False)

    pivot_start()
    load_own.start()

    @pl.when(has_rows)
    def _():
        load_rest.start()

    pivot_send(0)
    pivot_send(1)
    load_own.wait()
    pivot_end(0)
    pivot_step(0)
    pivot_send(2)
    panel_step(raw, a, a_hi, a_lo, 128, 128, 0)
    pivot_step(1)
    own_step(0)
    pivot_end(1)
    for j in range(2):
        panel_step(raw, a, a_hi, a_lo, BLK, BLK, j)
    pivot_step(2)
    forward_all(0)
    panel_step(raw, a, a_hi, a_lo, 384, 128, 2)
    pivot_step(3)
    own_step(1)
    pivot_end(2)
    for j in range(4):
        panel_step(raw, a, a_hi, a_lo, 2 * BLK, BLK, j)
    pivot_step(4)
    forward_all(1)
    own_step(2)
    panel_step(raw, a, a_hi, a_lo, 640, 128, 4)
    pivot_step(5)
    own_step(3)
    forward_all(2)

    def order(t):
        pair, by_row = (t - 1) // 2, lax.rem(t - 1, 2) == 0
        i = jnp.where(pair == 0, 1, jnp.where(pair == 1, 3, 2))
        u = t - 7
        dy = jnp.where(t == 0, 0, jnp.where(t < 7, jnp.where(by_row, 0, i), 1 + u // 3))
        dz = jnp.where(t == 0, 0, jnp.where(t < 7, jnp.where(by_row, i, 0), 1 + lax.rem(u, 3)))
        return lax.rem(y + dy, SIDE) * SIDE + lax.rem(z + dz, SIDE)

    whole = pl.ds(0, BLK)

    def x_copy(kind, c):
        source, rows, to = [
            (frame, whole, right), (frame, whole, left), (frame, whole, sibling),
            (left, pl.ds(0, HALF), right), (left, whole, sibling),
            (right, pl.ds(HALF, HALF), left), (right, whole, sibling),
            (across, whole, sibling),
        ][kind]
        dst = pieces.at[source, c, rows]
        src = chunk.at[c, rows] if kind < 3 else dst
        at = (near.at[c], near.at[c], late.at[0], far_sem.at[c], late.at[1], far_sem.at[c], late.at[2], late.at[3])
        return remote(src, dst, x_send.at[kind], at[kind], to, cell)

    def arrived(sem, region):
        remote(region, region, x_send.at[0], sem, sibling, cell).wait_recv()

    def keep(c):
        return pltpu.make_async_copy(chunk.at[c], pieces.at[frame, c], keep_sem)

    def step(t, carry):
        c = order(t)
        for n, i in enumerate(ORDER):
            @pl.when(t == 1 + n)
            def _(i=i):
                panel_forward(3, i, True)
                panel_forward(3, i, False)

        @pl.when((t < STEPS) & (c >= PB) & has_rows)
        def _():
            @pl.when(t == 0)
            def _():
                load_rest.wait()

            @pl.when(t >= 7)
            def _():
                part = held.at[:, c]
                remote(part, part, h_send.at[0, 0], h_recv.at[c], frame, cell).wait_recv()

            value = rest[:, pl.ds(pl.multiple_of((c - PB) * BLK, BLK), BLK)]
            for q in range(PB):
                value = value - lax.dot_general(
                    own_hi[:, BLK * q:BLK * (q + 1)], held[q, c], NT, preferred_element_type=F32
                )
            chunk[c] = value.astype(BF16)
            keep(c).start()
            for kind in range(3):
                x_copy(kind, c).start()

        back = order(t - LAG)

        @pl.when((t >= LAG) & (t < STEPS + LAG) & has_rows & (back >= PB))
        def _():
            arrived(near.at[back], pieces.at[pl.ds(0, 2), back])
            x_copy(3, back).start()
            x_copy(4, back).start()
            x_copy(5, back).start()
            x_copy(6, back).start()

        far = order(t - LAG2)

        @pl.when((t >= LAG2) & has_rows & (far >= PB))
        def _():
            arrived(far_sem.at[far], pieces.at[across, far])
            x_copy(7, far).start()

        return carry

    lax.fori_loop(0, STEPS + LAG2, step, 0)

    for r in range(PB):
        @pl.when(cell == r)
        def _(r=r):
            row_no = lax.broadcasted_iota(jnp.int32, (BLK, WIDTH), 0) + BLK * r
            col_no = lax.broadcasted_iota(jnp.int32, (BLK, WIDTH), 1)
            lower[...] = jnp.where(row_no >= col_no, a[BLK * r:BLK * (r + 1), :], 0.0)

    @pl.when(has_rows)
    def _():
        lower[...] = own[...]

    for r in range(PB):
        pivot_sent(r)
    for q, (_, wide) in enumerate(PANELS):
        @pl.when(has_rows)
        def _(q=q, wide=wide):
            part = held.at[0, pl.ds(0, 6), :, pl.ds(0, wide)]
            remote(part, part, l_send.at[q], l_recv.at[q, 0], frame, cell).wait_send()

        for count, when in (
            (9, (y != 0) & (z == SIDE - 1)), (6, (y != 0) & (z != SIDE - 1)),
            (3, (y == 0) & (z != SIDE - 1)),
        ):
            @pl.when(when)
            def _(q=q, count=count, wide=wide):
                part = held.at[0, pl.ds(0, count), pl.ds(0, HALF), pl.ds(0, wide)]
                for kind in range(2):
                    remote(part, part, h_send.at[q, kind], h_recv.at[0], frame, cell).wait_send()

    @pl.when(has_rows)
    def _():
        every = pl.ds(PB, CELLS - PB)
        full = pieces.at[frame, every]
        for n in range(4):
            arrived(late.at[n], full)
        pltpu.make_async_copy(chunk.at[every], full, keep_sem).wait()
        for kind in range(8):
            region = pieces.at[frame, every, pl.ds(0, HALF)] if kind in (3, 5) else full
            remote(region, region, x_send.at[kind], late.at[0], sibling, cell).wait_send()


def fronts(front):
    rest = CELLS * BLK - WIDTH
    return pl.pallas_call(
        fronts_kernel,
        out_shape=(
            jax.ShapeDtypeStruct((BLK, WIDTH), F32),
            jax.ShapeDtypeStruct((FRAMES, CELLS, BLK, BLK), BF16),
        ),
        in_specs=[pl.BlockSpec(memory_space=pl.ANY)],
        out_specs=(pl.BlockSpec(memory_space=VMEM), pl.BlockSpec(memory_space=pl.ANY)),
        scratch_shapes=[
            VMEM((WIDTH, WIDTH), F32), VMEM((WIDTH, WIDTH), F32),
            VMEM((WIDTH, WIDTH), BF16), VMEM((WIDTH, WIDTH), BF16),
            VMEM((BLK, WIDTH), F32), VMEM((BLK, WIDTH), BF16), VMEM((BLK, WIDTH), BF16),
            VMEM((WIDTH // 128, 128, 128), BF16), VMEM((WIDTH // 128, 128, 128), BF16),
            VMEM((128, 256), F32), VMEM((128, 256), F32),
            VMEM((PB, CELLS, BLK, BLK), BF16), VMEM((BLK, rest), F32), VMEM((CELLS, BLK, BLK), BF16),
            DMA((2,)), DMA((1,)), DMA((2, PB)), DMA((2,)), DMA((PB, 2)), DMA((PB, 2)),
            DMA((PB, 2)), DMA((PB,)),
            DMA((len(PANELS),)), DMA((len(PANELS), 6)), DMA((len(PANELS), 2)), DMA((CELLS,)),
            DMA((8,)), DMA((CELLS,)), DMA((CELLS,)), DMA((4,)), DMA,
        ],
        compiler_params=pltpu.CompilerParams(
            collective_id=1, has_side_effects=True, vmem_limit_bytes=56 << 20
        ),
        name="fronts",
    )(front)


GROUP = 4
SPAN = GROUP * BLK
WHOLE = CELLS // GROUP


def extend_kernel(parent_of, block_map, parent, pieces, out, total, buffer, table, sems):
    q, g = pl.program_id(0), pl.program_id(1)
    frame, cell = lax.axis_index("frame"), lax.axis_index("cell")
    turn = lax.rem(q, 2)

    @pl.when((q == 0) & (g == 0))
    def _():
        count, touched = 0, [0, 0]
        for c in range(FRAMES):
            live = ((parent_of[c] == frame) & (cell >= PB)).astype(jnp.int32)
            half = block_map[c, jnp.maximum(cell - PB, 0)] // CELLS
            table[count] = c
            table[CELLS + count] = half
            count = count + live
            touched = [touched[0] + live * (1 - half), touched[1] + live * half]
        table[2 * CELLS] = count
        table[2 * CELLS + 1], table[2 * CELLS + 2] = touched

    count = table[2 * CELLS]

    def fetch(n, at):
        slot = lax.rem(at, 2)
        return pltpu.make_async_copy(
            pieces.at[table[n], pl.ds(at * GROUP, GROUP)], buffer.at[slot, n], sems.at[slot, n]
        )

    def each(act):
        for n in range(FRAMES):
            @pl.when(n < count)
            def _(n=n):
                act(n)

    @pl.when((q == 0) & (g == 0))
    def _():
        each(lambda n: fetch(n, q).start())

    @pl.when((q + 1 < WHOLE) & (g == 0))
    def _():
        each(lambda n: fetch(n, q + 1).start())

    for h in range(2):
        used = table[2 * CELLS + 1 + h] > 0

        @pl.when(used)
        def _(h=h):
            total[h] = parent[h].astype(F32)

        @pl.when(jnp.logical_not(used))
        def _(h=h):
            out[h] = parent[h]

    @pl.when(g == 0)
    def _():
        each(lambda n: fetch(n, q).wait())

    def add(n):
        c, half = table[n], table[CELLS + n]
        for i in range(GROUP):
            block = q * GROUP + i

            @pl.when((block >= PB) & (block_map[c, jnp.maximum(block - PB, 0)] // CELLS == g))
            def _(i=i):
                total[half, :, i * BLK:(i + 1) * BLK] += buffer[turn, n, i].astype(F32)

    each(add)
    for h in range(2):
        @pl.when(table[2 * CELLS + 1 + h] > 0)
        def _(h=h):
            out[h] = total[h].astype(BF16)


def extend(parent_of, block_map, parent, pieces):
    tile = pl.BlockSpec((2, BLK, SPAN), lambda q, g, *_: (0, 0, g * WHOLE + q))
    return pl.pallas_call(
        extend_kernel,
        out_shape=jax.ShapeDtypeStruct(parent.shape, BF16),
        grid_spec=pltpu.PrefetchScalarGridSpec(
            num_scalar_prefetch=2,
            grid=(WHOLE, 2),
            in_specs=[tile, pl.BlockSpec(memory_space=pl.ANY)],
            out_specs=tile,
            scratch_shapes=[
                VMEM((2, BLK, SPAN), F32), VMEM((2, FRAMES, GROUP, BLK, BLK), BF16),
                pltpu.SMEM((3 * CELLS,), jnp.int32), DMA((2, FRAMES)),
            ],
        ),
        compiler_params=pltpu.CompilerParams(vmem_limit_bytes=60 << 20),
        name="extend",
    )(parent_of, block_map, parent, pieces)


def per_device(front, parent_of, block_map, parent_in):
    lower, pieces = fronts(front[0])
    out = extend(parent_of, block_map, parent_in[0], pieces)
    return lower[None], out[None]


def solution(mesh):
    placed = (P("frame", "cell", None), P(), P(), P("frame", None, "cell", None))
    return jax.shard_map(
        per_device,
        mesh=mesh,
        in_specs=placed,
        out_specs=(P("frame", "cell", None), P("frame", None, "cell", None)),
        check_vma=False,
    )
```

time: 148 us -> 143 us (0.966)
  Pallas kernels: 145 us -> 140 us
    pallas_call x1, Pallas kernels: 133 us -> 128 us  [fronts(): pl.pallas_call(fronts_kernel, out_shape=(jax.ShapeDtypeStruct((BLK, WIDTH...]
where the time goes in v3:
time: 143 us; the launch traced here: 141 us
  Pallas kernels  140 us (98%)
    pallas_call x1, Pallas kernels, fronts(): pl.pallas_call(fronts_kernel, out_shape=(jax.ShapeDtypeStruct((BLK, WIDTH...  128 us
    pallas_call x1, Pallas kernels, extend(): pl.pallas_call(extend_kernel, out_shape=jax.ShapeDtypeStruct(parent.shape...  12 us

profile of v3, /device:TPU:15, one launch (start us, length us, event | category | flops | bytes accessed | tf_op | source)
XLA Modules:
  0.0 141.1 jit_solution(17449687719704147023)
XLA Ops:
  0.6 127.6 %fronts.1 = (f32[256,768]{1,0:T(8,128)}, bf16[8,16,256,256]{3,2,1,0:T(8,128)(2,1)}) custom-call(f32[256,4096]{1,0:T(8,128)} %bitcast.6), custom_call_target="tpu_custom_call" | custom-call | tf_op jit(solution)/shard_map/fronts/pallas_call | solution.py:452
  128.2 0.0 copy-start
  128.2 12.0 %extend.1 = bf16[2,256,8192]{2,1,0:T(8,128)(2,1)} custom-call(s32[8]{0:T(128)} %parent_of.1, s32[8,13]{1,0:T(8,128)} %block_map.1, bf16[2,256,8192]{2,1,0:T(8,128)(2,1)} %bitcast.4, bf16[8,16,256,256]{3,2,1,0:T(8,128)(2,1)} %get-tuple-element.5.pieces), custom_call_target="tpu_custom_call" | custom-call | tf_op jit(solution)/shard_map/extend/pallas_call | solution.py:557
  140.2 0.0 copy-done
  140.2 0.9 copy.7
Async XLA Ops:
  128.2 12.0 %copy-start = (f32[256,768]{1,0:T(8,128)S(1)}, f32[256,768]{1,0:T(8,128)}, u32[]{:S(2)}) copy-start(f32[256,768]{1,0:T(8,128)} %get-tuple-element.4) | copy-start | bytes 2359300
